TPU v7x, 32 devices: a whole 2x2x4 slice. The times are simulated.
32 devices in a mesh: grp: 2 (over y), store: 8 (over z, core), tp: 2 (over x).
Axes of the slice: x: 2, y: 2, z: 4, core: 2. Of those that a mesh axis runs over, the one named last changes fastest.
Arguments:
- tokens: bfloat16 [10240, 8192], P(('grp', 'store'), 'tp'), parts along dimension 0, may hold values from -6 to 6
- value_matrix: bfloat16 [8192, 1024], P('tp'), may hold values from -0.0625 to 0.0625
- adapter_down_matrix: bfloat16 [64, 8192, 128], P(('grp', 'store'), 'tp'), parts along dimension 0, may hold values from -0.0625 to 0.0625
- adapter_up_matrix: bfloat16 [64, 128, 1024], P(('grp', 'store'), None, 'tp'), parts along dimension 0, may hold values from -0.5 to 0.5
- adapter_rank_list: int32 [64], P('grp'), parts along dimension 0, may hold values from 16 to 128
- requests: int32 [16, 4], P(('grp', 'store')), parts along dimension 0, may hold values from 0 to 31, as said below
- segment_row_lengths: int32 [16, 4], P(('grp', 'store')), parts along dimension 0, may hold values from 1 to 320, 640 in all within a row
Outputs:
- adapted_values: bfloat16 [10240, 1024], P(('grp', 'store'), 'tp'), parts along dimension 0
There are 2 independent parts, one for each index of `grp`. A program takes and returns all parts, laid end to end along the dimension named above; an argument that names none is the same for every part. Nothing has to cross between parts.
Inputs may be any that keep to these rules, and one draw needn't show every extreme that they name: `requests`: entry (j, s) names the adapter of segment s of instance j; adapter a is stored at index a // 4 of store, and the 4 adapters of one instance are stored on 4 different indices of store. `segment_row_lengths`: each instance's 4 lengths sum to 640.
All inputs are finite; a program needn't handle non-finite values.
Results may differ from a plain program's by a relative error of at most 0.0034.
Values may be sent and summed in bfloat16 or wider, within the bound.
A program may use at most 128 MiB of HBM per device.

v0:
```python
import jax
import jax.numpy as jnp
from jax import lax
from jax.sharding import PartitionSpec as P

adapter_alpha = 32.0


def segment_layout(lengths, segment_capacity, row_count, mixture_count):
    starts = jnp.cumsum(lengths) - lengths
    step_ids = jnp.arange(segment_capacity, dtype=jnp.int32)
    window_index = jnp.minimum(starts[:, None] + step_ids[None, :], row_count - 1)
    row_ids = jnp.arange(row_count, dtype=jnp.int32)
    segment_piece = jnp.sum((starts[None, :] <= row_ids[:, None]).astype(jnp.int32), axis=1) - 1
    is_segment = segment_piece[:, None] == jnp.arange(mixture_count, dtype=jnp.int32)[None, :]
    start_of = jnp.sum(jnp.where(is_segment, starts[None, :], 0), axis=1)
    return (window_index, segment_piece * segment_capacity + (row_ids - start_of))


def column_gain(adapter_rank_list, desired_identifiers, highest_rank):
    table_ids = jnp.arange(adapter_rank_list.shape[0], dtype=jnp.int32)
    chosen_ranks = jnp.sum(
        jnp.where(
            desired_identifiers[:, None] == table_ids[None, :], adapter_rank_list[None, :], 0
        ),
        axis=1,
    )
    column_ids = jnp.arange(highest_rank, dtype=jnp.int32)
    retained_columns = (column_ids[None, :] < chosen_ranks[:, None]).astype(jnp.float32)
    return retained_columns * (adapter_alpha / chosen_ranks.astype(jnp.float32))[:, None]


def local(
    tokens,
    value_matrix,
    adapter_down_matrix,
    adapter_up_matrix,
    adapter_rank_list,
    requests,
    segment_row_lengths,
):
    row_count = tokens.shape[0]
    adapter_tally = adapter_down_matrix.shape[0]
    highest_rank = adapter_down_matrix.shape[2]
    mixture_count = requests.shape[1]
    segment_capacity = 2 * row_count // max(mixture_count, 4)
    base_part = jnp.dot(tokens, value_matrix, preferred_element_type=jnp.float32)
    base_values = lax.psum_scatter(base_part, "tp", scatter_dimension=1, tiled=True)
    desired_identifiers = requests[0]
    window_index, row_slot = segment_layout(
        segment_row_lengths[0], segment_capacity, row_count, mixture_count
    )
    segment_spans = tokens[window_index]
    owner_of = desired_identifiers // adapter_tally
    every_request = lax.all_gather(requests, "store", axis=0, tiled=True)
    my_owner = lax.axis_index("store")
    is_mine = every_request // adapter_tally == my_owner
    nearby_position = jnp.sum(
        jnp.where(is_mine, every_request - my_owner * adapter_tally, 0), axis=1
    )
    pulled_down, pulled_up = (
        lax.all_to_all(
            adapter_down_matrix[nearby_position], "store", split_axis=0, concat_axis=0, tiled=True
        ),
        lax.all_to_all(
            adapter_up_matrix[nearby_position], "store", split_axis=0, concat_axis=0, tiled=True
        ),
    )
    segment_down = pulled_down[owner_of]
    segment_up = pulled_up[owner_of]
    adapter_middle = jnp.einsum(
        "kng,kgz->knz", segment_spans, segment_down, preferred_element_type=jnp.float32
    )
    adapter_middle = lax.psum(adapter_middle, "tp")
    column_factors = column_gain(adapter_rank_list, desired_identifiers, highest_rank)
    scaled_update = (adapter_middle * column_factors[:, None, :]).astype(jnp.bfloat16)
    adapter_update = jnp.einsum(
        "poa,pal->pol", scaled_update, segment_up, preferred_element_type=jnp.float32
    )
    flattened_delta = adapter_update.reshape(
        mixture_count * segment_capacity, adapter_update.shape[2]
    )
    return (base_values + flattened_delta[row_slot]).astype(jnp.bfloat16)


def solution(mesh):
    in_specs = (
        P(("grp", "store"), "tp"),
        P("tp", None),
        P(("grp", "store"), "tp", None),
        P(("grp", "store"), None, "tp"),
        P("grp"),
        P(("grp", "store"), None),
        P(("grp", "store"), None),
    )
    out_specs = P(("grp", "store"), "tp")
    return jax.shard_map(local, mesh=mesh, in_specs=in_specs, out_specs=out_specs, check_vma=False)
```

profile of v0, /device:TPU:0, one launch (start us, length us, event | category | flops | bytes accessed | tf_op | source)
XLA Modules:
  0.0 311.7 jit_solution(13696196303305392538)
XLA Ops:
  6.5 0.0 copy-start
  6.5 13.7 %all-gather = s32[8,1,4]{2,1,0:T(1,128)S(1)} all-gather(s32[1,1,4]{2,1,0:T(1,128)} %bitcast.63), channel_id=1, replica_groups=mesh['grp'=2,'store'=8,'tp'=2] {'store'}, dimensions={0}, use_global_device_ids=true | all-gather | bytes 144 | tf_op jit(solution)/shard_map/all_gather | solution.py:55
  20.2 0.1 copy.11
  20.3 6.8 %gather_fusion.1 = bf16[8,4096,128]{2,1,0:T(8,128)(2,1)} fusion(bf16[4,4096,128]{2,1,0:T(8,128)(2,1)} %param.9, s32[1024]{0:T(1024)S(1)} %pad_clamp_fusion.3), kind=kCustom, calls=%fused_computation.1 | custom fusion | bytes 16777248 | tf_op jit(solution)/shard_map/gather | solution.py:63
  27.1 0.0 copy-start.2
  27.1 5.1 %all-to-all-start = ((bf16[8,4096,128]{2,1,0:T(8,128)(2,1)}), bf16[8,4096,128]{2,1,0:T(8,128)(2,1)}, u32[]{:S(2)}, u32[]{:S(2)}) async-start(bf16[8,4096,128]{2,1,0:T(8,128)(2,1)} %gather_fusion.1), calls=%async_computation.1 | async-start | bytes 16777216 | tf_op jit(solution)/shard_map/all_to_all | solution.py:62
  32.2 0.0 all-reduce.2.cloned.1.call-start
  32.3 0.0 copy-done.2
  32.3 0.2 reduce-window.4
  32.5 0.1 compare_select_fusion
  32.5 0.1 reshape.237
  32.6 0.0 copy-start.1
  32.6 21.9 %gather_fusion = bf16[1280,4096]{1,0:T(8,128)(2,1)} fusion(bf16[640,4096]{1,0:T(8,128)(2,1)} %param.7, s32[2048]{0:T(1024)S(1)} %pad_clamp_fusion), kind=kCustom, calls=%fused_computation | custom fusion | bytes 20976640 | tf_op jit(solution)/shard_map/gather | solution.py:53
  54.6 0.0 copy-done.1
  54.6 161.5 %all-to-all-done = bf16[8,4096,128]{2,1,0:T(8,128)(2,1)} async-done(((bf16[8,4096,128]{2,1,0:T(8,128)(2,1)}), bf16[8,4096,128]{2,1,0:T(8,128)(2,1)}, u32[]{:S(2)}, u32[]{:S(2)}) %all-to-all-start) | async-done | bytes 8388640 | tf_op jit(solution)/shard_map/all_to_all | solution.py:62
  216.1 6.5 %gather_fusion.2 = bf16[4,4096,128]{2,1,0:T(8,128)(2,1)} fusion(bf16[8,4096,128]{2,1,0:T(8,128)(2,1)} %all-to-all-done, s32[1024]{0:T(1024)S(1)} %pad_clamp_fusion.2), kind=kCustom, calls=%fused_computation.2 | custom fusion | bytes 8388624 | tf_op jit(solution)/shard_map/gather | solution.py:69
  222.6 9.0 %fusion.14 = f32[4,320,128]{2,1,0:T(8,128)} fusion(bf16[4,320,4096]{2,1,0:T(8,128)(2,1)} %bitcast.62, bf16[4,4096,128]{2,1,0:T(8,128)(2,1)} %gather_fusion.2), kind=kOutput, calls=%fused_computation.54 | convolution fusion | flops 1342177280 | bytes 15335424 | tf_op jit(solution)/shard_map/kng,kgz->knz/dot_general | solution.py:71
  231.6 0.0 all-reduce.2.cloned.1.call-update
  231.6 0.0 reduce-scatter.2.cloned.1.call-start
  231.6 10.6 %fusion.13 = f32[640,1024]{1,0:T(8,128)} fusion(bf16[640,4096]{1,0:T(8,128)(2,1)} %param.7, bf16[4096,1024]{1,0:T(8,128)(2,1)} %param.8), kind=kOutput, calls=%fused_computation.53 | convolution fusion | flops 5368709120 | bytes 16252928 | tf_op jit(solution)/shard_map/dot_general | solution.py:47
  242.2 0.0 copy-start.3
  242.2 0.0 reduce-scatter.2.cloned.1.call-update
  242.2 0.0 copy-done
  242.3 1.6 gather_fusion.3
  243.9 3.6 %all-to-all-start.1 = ((bf16[8,128,512]{2,1,0:T(8,128)(2,1)}), bf16[8,128,512]{2,1,0:T(8,128)(2,1)S(1)}, u32[]{:S(2)}, u32[]{:S(2)}) async-start(bf16[8,128,512]{2,1,0:T(8,128)(2,1)} %gather_fusion.3), calls=%async_computation.2 | async-start | bytes 2097152 | tf_op jit(solution)/shard_map/all_to_all | solution.py:65
  247.4 0.1 convert_reduce_fusion
  247.5 0.1 select_reduce_fusion
  247.7 0.0 copy-done.3
  247.7 0.2 select_reduce_fusion.1
  247.9 0.1 fusion.8
  247.9 26.0 %all-to-all-done.1 = bf16[8,128,512]{2,1,0:T(8,128)(2,1)S(1)} async-done(((bf16[8,128,512]{2,1,0:T(8,128)(2,1)}), bf16[8,128,512]{2,1,0:T(8,128)(2,1)S(1)}, u32[]{:S(2)}, u32[]{:S(2)}) %all-to-all-start.1) | async-done | bytes 1048608 | tf_op jit(solution)/shard_map/all_to_all | solution.py:65
  273.9 1.4 gather_fusion.4
  275.3 0.0 all-reduce.2.cloned.1.call-done
  275.3 1.7 fusion
  277.0 3.0 gather_fusion.5
  280.1 22.0 %reduce-scatter.2.cloned.1.call-done = f32[640,512]{1,0:T(8,128)} async-done(((f32[640,1024]{1,0:T(8,128)}), f32[640,512]{1,0:T(8,128)}) %reduce-scatter.2.cloned.1.call-update) | async-done | bytes 1310736 | tf_op jit(solution)/shard_map/reduce_scatter | solution.py:48
  302.1 2.7 add_convert_fusion
  (12 shorter events, 0.1 us)
Async XLA Ops:
  6.5 235.7 %copy-start = (bf16[4,128,512]{2,1,0:T(8,128)(2,1)S(1)}, bf16[4,128,512]{2,1,0:T(8,128)(2,1)}, u32[]{:S(2)}) copy-start(bf16[4,128,512]{2,1,0:T(8,128)(2,1)} %param.10) | copy-start | bytes 1572868
  27.1 5.1 %copy-start.2 = (s32[1,4]{1,0:T(1,128)S(1)}, s32[1,4]{1,0:T(1,128)}, u32[]{:S(2)}) copy-start(s32[1,4]{1,0:T(1,128)} %param.13) | copy-start | bytes 52
  27.1 189.0 %all-to-all-start = ((bf16[8,4096,128]{2,1,0:T(8,128)(2,1)}), bf16[8,4096,128]{2,1,0:T(8,128)(2,1)}, u32[]{:S(2)}, u32[]{:S(2)}) async-start(bf16[8,4096,128]{2,1,0:T(8,128)(2,1)} %gather_fusion.1), calls=%async_computation.1 | async-start | bytes 16777216 | tf_op jit(solution)/shard_map/all_to_all | solution.py:62
  32.2 243.1 %all-reduce.2.cloned.1.call-start = ((), (), s32[]{:S(2)}) async-start(), calls=%async_computation.4 | async-start | bytes 1310720 | tf_op jit(solution)/shard_map/psum | solution.py:74
  32.6 21.9 %copy-start.1 = (s32[1,4]{1,0:T(1,128)S(1)}, s32[1,4]{1,0:T(1,128)}, u32[]{:S(2)}) copy-start(s32[1,4]{1,0:T(1,128)} %param.12) | copy-start | bytes 52
  231.6 70.5 %reduce-scatter.2.cloned.1.call-start = ((), (), s32[]{:S(2)}) async-start(), calls=%async_computation.3 | async-start | bytes 3932160 | tf_op jit(solution)/shard_map/reduce_scatter | solution.py:48
  242.2 5.4 %copy-start.3 = (s32[32]{0:T(128)S(1)}, s32[32]{0:T(128)}, u32[]{:S(2)}) copy-start(s32[32]{0:T(128)} %param.11) | copy-start | bytes 388
  243.9 30.1 %all-to-all-start.1 = ((bf16[8,128,512]{2,1,0:T(8,128)(2,1)}), bf16[8,128,512]{2,1,0:T(8,128)(2,1)S(1)}, u32[]{:S(2)}, u32[]{:S(2)}) async-start(bf16[8,128,512]{2,1,0:T(8,128)(2,1)} %gather_fusion.3), calls=%async_computation.2 | async-start | bytes 2097152 | tf_op jit(solution)/shard_map/all_to_all | solution.py:65
Sparse Core Ops, SparseCore 0:
  231.7 30.4 all-reduce.1
  264.5 37.5 reduce-scatter.1
where the time goes:
time: 312 us
  waiting for transfers between devices  210 us (67%)
  local copies, waits for them, and re-layouts  41.4 us (13%)
  matrix products  21.3 us (7%)
  blocking collectives  13.7 us (4%)
  between operations  13.5 us (4%)
  starting transfers between devices  8.72 us (3%)
  other arithmetic  3.54 us (1%)
    all_to_all x1, waiting for transfers between devices, local(): lax.all_to_all(adapter_down_matrix[nearby_position], 'store', split_axis=...  162 us
    all_to_all x1, waiting for transfers between devices, local(): lax.all_to_all(adapter_up_matrix[nearby_position], 'store', split_axis=0,...  26 us
    reduce_scatter x1, waiting for transfers between devices, local(): lax.psum_scatter(base_part, 'tp', scatter_dimension=1, tiled=True)  22 us
    gather x1, local copies, waits for them, and re-layouts, local(): segment_spans = tokens[window_index]  21.9 us
    all_gather x1, blocking collectives, local(): every_request = lax.all_gather(requests, 'store', axis=0, tiled=True)  13.7 us
    dot_general x1, matrix products, local(): jnp.dot(tokens, value_matrix, preferred_element_type=jnp.float32)  10.6 us
    dot_general x1, matrix products, local(): jnp.einsum('kng,kgz->knz', segment_spans, segment_down, preferred_element...  8.95 us
    gather x1, local copies, waits for them, and re-layouts, local(): adapter_down_matrix[nearby_position]  6.8 us
  transfers between devices with their start and end apart: 4, of which 3 were waited for; matrix products, arithmetic and copies ran while one was open for 13% of the time, Pallas kernels for 0%

commit v1 on v0

--- a/solution.py
+++ b/solution.py
@@ -1,9 +1,12 @@
+import functools
+
 import jax
 import jax.numpy as jnp
 from jax import lax
 from jax.sharding import PartitionSpec as P
 
 adapter_alpha = 32.0
+CAPACITY_PARTS = (4, 5, 6, 8, 16)
 
 
 def segment_layout(lengths, segment_capacity, row_count, mixture_count):
@@ -82,6 +85,216 @@
     )
     return (base_values + flattened_delta[row_slot]).astype(jnp.bfloat16)
 
+def exclusive_sum(lens):
+    return jnp.cumsum(lens, axis=-1) - lens
+
+
+def one_hot_rows(height, source):
+    q = lax.broadcasted_iota(jnp.int32, (height, source.shape[0]), 0)
+    return (q == source[None, :]).astype(jnp.bfloat16)
+
+
+def copy_columns(values, chosen):
+    return jnp.dot(values, chosen, preferred_element_type=jnp.float32)
+
+
+def exchange_sum(x, n_tp):
+    if n_tp != 2:
+        return lax.psum(x, "tp")
+    return x + lax.ppermute(x, "tp", [(0, 1), (1, 0)])
+
+
+def link_tables(asked, ranks, n_chips, owner_chip):
+    dest = jnp.arange(n_chips, dtype=jnp.int32)
+    right, left = [], []
+    for z in range(n_chips):
+        beyond = jnp.any(asked & (dest > z)[:, None], axis=0) & (owner_chip <= z)
+        right.append(jnp.where(beyond, ranks, 0))
+        before = jnp.any(asked & (dest < z)[:, None], axis=0) & (owner_chip >= z)
+        left.append(jnp.where(before, ranks, 0))
+    return jnp.stack(right), jnp.stack(left)
+
+
+def hop_plan(
+    capacity,
+    n_store,
+    n_tp,
+    tokens,
+    value_matrix,
+    down,
+    up,
+    ranks,
+    all_requests,
+    lengths,
+    right_lens,
+    left_lens,
+):
+    rows, feats = tokens.shape
+    per_dev, _, rank_cap = down.shape
+    outs = up.shape[2]
+    n_seg = all_requests.shape[1]
+    n_chips = n_store // 2
+    own_width = 2 * per_dev * rank_cap
+    half = feats // 2 + outs // 2
+    depth = next(d for d in (384, 256, 128, 64, 32, 16, half) if half % d == 0)
+    chunks = half // depth
+    store = lax.axis_index("store")
+    z, core = store // 2, lax.rem(store, 2)
+    swap = [(i, i ^ 1) for i in range(n_store)]
+    rightward = [(i, i + 2) for i in range(n_store - 2)]
+    leftward = [(i + 2, i) for i in range(n_store - 2)]
+
+    down_rows = down.transpose(1, 0, 2).reshape(2, feats // 2, per_dev * rank_cap)
+    up_rows = up.transpose(2, 0, 1).reshape(2, outs // 2, per_dev * rank_cap)
+    both = jnp.concatenate([down_rows, up_rows], axis=1)
+    mine = lax.dynamic_index_in_dim(both, core, 0, keepdims=False)
+    given = lax.dynamic_index_in_dim(both, 1 - core, 0, keepdims=False)
+    got = lax.ppermute(given, "store", swap)
+    first = core == 0
+    own = jnp.concatenate([jnp.where(first, mine, got), jnp.where(first, got, mine)], axis=1)
+
+    ids = jnp.arange(ranks.shape[0], dtype=jnp.int32)
+    owner_chip = ids // (2 * per_dev)
+    own_at = (ids - z * 2 * per_dev) * rank_cap
+    is_own = owner_chip == z
+    right_at, left_at = exclusive_sum(right_lens), exclusive_sum(left_lens)
+
+    def row_of(table, at):
+        return lax.dynamic_index_in_dim(table, jnp.clip(at, 0, n_chips - 1), 0, keepdims=False)
+
+    in_right_at, in_left_at = row_of(right_at, z - 1), row_of(left_at, z + 1)
+    spots = jnp.arange(capacity, dtype=jnp.int32)
+
+    def forward(lens, out_at, in_at):
+        active = (out_at[:, None] <= spots) & (spots < (out_at + lens)[:, None])
+        offset = spots[None, :] - out_at[:, None]
+
+        def source(kept, base):
+            taken = active & kept[:, None]
+            return jnp.sum(jnp.where(taken, offset + base[:, None] + 1, 0), axis=0) - 1
+
+        return (
+            one_hot_rows(own_width, source(is_own, own_at)),
+            one_hot_rows(capacity, source(~is_own, in_at)),
+        )
+
+    own_r, pass_r = forward(row_of(right_lens, z), row_of(right_at, z), in_right_at)
+    own_l, pass_l = forward(row_of(left_lens, z), row_of(left_at, z), in_left_at)
+
+    columns = jnp.arange(rank_cap, dtype=jnp.int32)
+
+    def extract(instance):
+        wanted = lax.dynamic_index_in_dim(all_requests, instance, 0, keepdims=False)
+        is_it = wanted[:, None] == ids[None, :]
+
+        def source(kept, base):
+            at = jnp.sum(jnp.where(is_it & kept[None, :], base[None, :] + 1, 0), axis=1) - 1
+            size = jnp.sum(jnp.where(is_it & kept[None, :], ranks[None, :], 0), axis=1)
+            spot = jnp.where(columns[None, :] < size[:, None], at[:, None] + columns[None, :], -1)
+            return spot.reshape(n_seg * rank_cap)
+
+        return (
+            source(is_own, own_at),
+            source(owner_chip < z, in_right_at),
+            source(owner_chip > z, in_left_at),
+        )
+
+    sib, my = extract(z * 2 + 1 - core), extract(store)
+    take_own, take_r, take_l = (
+        one_hot_rows(height, jnp.concatenate([sib[i], my[i]]))
+        for i, height in enumerate((own_width, capacity, capacity))
+    )
+    start_r = copy_columns(own, own_r).astype(jnp.bfloat16)
+    start_l = copy_columns(own, own_l).astype(jnp.bfloat16)
+
+    steps = chunks + n_chips - 2
+    in_r = in_l = None
+    parts_r, parts_l = [], []
+    for t in range(steps):
+        at_r = jnp.clip(t - z, 0, chunks - 1) * depth
+        at_l = jnp.clip(t - (n_chips - 1 - z), 0, chunks - 1) * depth
+        send_r = lax.dynamic_slice_in_dim(start_r, at_r, depth, 0)
+        send_l = lax.dynamic_slice_in_dim(start_l, at_l, depth, 0)
+        if t > 0:
+            send_r = (send_r + copy_columns(in_r, pass_r)).astype(jnp.bfloat16)
+            send_l = (send_l + copy_columns(in_l, pass_l)).astype(jnp.bfloat16)
+        in_r = lax.ppermute(send_r, "store", rightward)
+        in_l = lax.ppermute(send_l, "store", leftward)
+        parts_r.append(copy_columns(in_r, take_r).astype(jnp.bfloat16))
+        parts_l.append(copy_columns(in_l, take_l).astype(jnp.bfloat16))
+    base = jnp.dot(tokens, value_matrix, preferred_element_type=jnp.float32)
+    if n_tp == 2:
+        tp = lax.axis_index("tp")
+        far = lax.dynamic_slice_in_dim(base, (1 - tp) * outs, outs, 1)
+        near = lax.dynamic_slice_in_dim(base, tp * outs, outs, 1)
+        base_values = near + lax.ppermute(far, "tp", [(0, 1), (1, 0)])
+    else:
+        base_values = lax.psum_scatter(base, "tp", scatter_dimension=1, tiled=True)
+    from_r = lax.dynamic_slice_in_dim(
+        jnp.concatenate(parts_r, 0), jnp.clip(z - 1, 0, n_chips - 2) * depth, half, 0
+    )
+    from_l = lax.dynamic_slice_in_dim(
+        jnp.concatenate(parts_l, 0), jnp.clip(n_chips - 2 - z, 0, n_chips - 2) * depth, half, 0
+    )
+    from_own = copy_columns(own, take_own).astype(jnp.bfloat16)
+    found = from_own + jnp.where(z > 0, from_r, 0) + jnp.where(z < n_chips - 1, from_l, 0)
+    wide = n_seg * rank_cap
+    here = found[:, wide:]
+    there = lax.ppermute(found[:, :wide], "store", swap)
+    low, high = jnp.where(first, here, there), jnp.where(first, there, here)
+    cut = feats // 2
+    inner = jnp.dot(tokens[:, :cut], low[:cut], preferred_element_type=jnp.float32)
+    inner = inner + jnp.dot(tokens[:, cut:], high[:cut], preferred_element_type=jnp.float32)
+    starts = exclusive_sum(lengths)
+    row_ids = jnp.arange(rows, dtype=jnp.int32)
+    inside = (starts[None, :] <= row_ids[:, None]) & (
+        row_ids[:, None] < (starts + lengths)[None, :]
+    )
+    inner = jnp.sum(jnp.where(inside[:, :, None], inner.reshape(rows, n_seg, rank_cap), 0.0), axis=1)
+    inner = exchange_sum(inner, n_tp)
+    my_request = lax.dynamic_index_in_dim(all_requests, store, 0, keepdims=False)
+    factors = column_gain(ranks, my_request, rank_cap)
+    scaled = (inner[:, None, :] * factors[None, :, :]).astype(jnp.bfloat16)
+    scaled = jnp.where(inside[:, :, None], scaled, 0).reshape(rows, wide)
+    up_all = jnp.concatenate([low[cut:], high[cut:]], axis=0)
+    delta = lax.dot_general(
+        scaled, up_all, (((1,), (1,)), ((), ())), preferred_element_type=jnp.float32
+    )
+    return (base_values + delta).astype(jnp.bfloat16)
+
+
+def by_hops(n_grp, n_store, n_tp, tokens, value_matrix, down, up, rank_list, requests, lengths):
+    n_chips, per_dev, rank_cap = n_store // 2, down.shape[0], down.shape[2]
+    n_seg = requests.shape[1]
+    n_adapters = n_store * per_dev
+    store, grp = lax.axis_index("store"), lax.axis_index("grp")
+    my_ranks = lax.dynamic_slice_in_dim(rank_list, store * per_dev, per_dev, 0)
+    note = jnp.concatenate([requests[0], my_ranks])[None, :]
+    notes = lax.all_gather(note, ("grp", "store"), axis=0, tiled=True)
+    notes = notes.reshape(n_grp, n_store, n_seg + per_dev)
+    ids = jnp.arange(n_adapters, dtype=jnp.int32)
+    owner_chip = ids // (2 * per_dev)
+    tables, load = [], 0
+    for g in range(n_grp):
+        asked = notes[g, :, :n_seg].reshape(n_chips, 2 * n_seg)
+        asked = jnp.any(asked[:, :, None] == ids[None, None, :], axis=1)
+        ranks = notes[g, :, n_seg:].reshape(n_adapters)
+        right, left = link_tables(asked, ranks, n_chips, owner_chip)
+        tables.append(jnp.stack([right, left]))
+        load = jnp.maximum(load, jnp.max(jnp.sum(tables[-1], axis=-1)))
+    mine = lax.dynamic_index_in_dim(jnp.stack(tables), grp, 0, keepdims=False)
+    all_requests = lax.dynamic_index_in_dim(notes[:, :, :n_seg], grp, 0, keepdims=False)
+    most = n_chips * per_dev * rank_cap
+    sizes = [most * part // 16 for part in CAPACITY_PARTS]
+    branches = [
+        lambda *ops, size=size: hop_plan(size, n_store, n_tp, *ops) for size in sizes
+    ]
+    branch = sum((load > size).astype(jnp.int32) for size in sizes[:-1])
+    return lax.switch(
+        branch, branches, tokens, value_matrix, down, up, rank_list, all_requests,
+        lengths[0], mine[0], mine[1],
+    )
+
 
 def solution(mesh):
     in_specs = (
@@ -94,4 +307,8 @@
         P(("grp", "store"), None),
     )
     out_specs = P(("grp", "store"), "tp")
-    return jax.shard_map(local, mesh=mesh, in_specs=in_specs, out_specs=out_specs, check_vma=False)
+    n_grp, n_store, n_tp = (mesh.shape[axis] for axis in ("grp", "store", "tp"))
+    body = local
+    if n_store % 2 == 0 and 4 <= n_store <= 8:
+        body = functools.partial(by_hops, n_grp, n_store, n_tp)
+    return jax.shard_map(body, mesh=mesh, in_specs=in_specs, out_specs=out_specs, check_vma=False)

time: 312 us -> 266 us (0.85)
  waiting for transfers between devices: 210 us -> 82.4 us
  starting transfers between devices: 8.72 us -> 46.9 us
  matrix products: 21.3 us -> 54 us
  loops' own time: 0 us -> 19 us
  between operations: 13.5 us -> 2.64 us
  local copies, waits for them, and re-layouts: 41.4 us -> 34.8 us
  other arithmetic: 3.54 us -> 9.87 us
    all_to_all x2 -> x0, waiting for transfers between devices: 188 us -> none  [the longest x1 162 us: local(): lax.all_to_all(adapter_down_matrix[nearby_position], 'store', split_axis=...]
    ppermute x0 -> x20, waiting for transfers between devices: none -> 82.4 us  [the longest x8 30.2 us: hop_plan(): in_r = lax.ppermute(send_r, 'store', rightward)]
    ppermute x0 -> x20, starting transfers between devices: none -> 46.9 us  [the longest x8 34 us: hop_plan(): in_r = lax.ppermute(send_r, 'store', rightward)]
    gather x6 -> x0, local copies, waits for them, and re-layouts: 41.2 us -> none  [the longest x1 21.9 us: local(): segment_spans = tokens[window_index]]
    dot_general x3 -> x37, matrix products: 21.3 us -> 54 us  [the longest x33 38.8 us: copy_columns(): return jnp.dot(values, chosen, preferred_element_type=jnp.float32)]
    reduce_scatter x1 -> x0, waiting for transfers between devices: 22 us -> none  [local(): lax.psum_scatter(base_part, 'tp', scatter_dimension=1, tiled=True)]
    unnamed x0 -> x1, loops' own time: none -> 19 us
    unnamed x0 -> x1, blocking collectives: none -> 13.7 us
  transfers between devices with their start and end apart: 4 -> 20, of which waited for: 3 -> 18; matrix products, arithmetic and copies ran while one was open for 13% -> 18% of each run, Pallas kernels for 0% -> 0%
where the time goes in v1:
time: 266 us; the launch traced here: 263 us
  waiting for transfers between devices  82.4 us (31%)
  matrix products  54 us (20%)
  starting transfers between devices  46.9 us (18%)
  local copies, waits for them, and re-layouts  34.8 us (13%)
  loops' own time  19 us (7%)
  blocking collectives  13.7 us (5%)
  other arithmetic  9.87 us (4%)
    dot_general x33, matrix products, copy_columns(): return jnp.dot(values, chosen, preferred_element_type=jnp.float32)  38.8 us
    ppermute x8, starting transfers between devices, hop_plan(): in_r = lax.ppermute(send_r, 'store', rightward)  34 us
    ppermute x8, waiting for transfers between devices, hop_plan(): in_r = lax.ppermute(send_r, 'store', rightward)  30.2 us
    ppermute x1, waiting for transfers between devices, exchange_sum(): return x + lax.ppermute(x, 'tp', [(0, 1), (1, 0)])  26.9 us
    ppermute x8, waiting for transfers between devices, hop_plan(): in_l = lax.ppermute(send_l, 'store', leftward)  22.5 us
    unnamed x1, loops' own time  19 us
    unnamed x1, blocking collectives  13.7 us
    unnamed x23, local copies, waits for them, and re-layouts  11.3 us
  transfers between devices with their start and end apart: 20, of which 18 were waited for; matrix products, arithmetic and copies ran while one was open for 18% of the time, Pallas kernels for 0%

profile of v1, /device:TPU:0, one launch (start us, length us, event | category | flops | bytes accessed | tf_op | source)
XLA Modules:
  0.0 263.3 jit_solution(3959848916701778023)
XLA Ops:
  0.7 1.2 dynamic-slice.30
  3.5 13.7 %all-reduce = s32[128]{0:T(128)S(1)} all-reduce(s32[128]{0:T(128)S(1)} %add_dynamic-update-slice_fusion), channel_id=2, replica_groups=mesh['grp'=2,'store'=8,'tp'=2] {'grp','store'}, use_global_device_ids=true, to_apply=%add | all-reduce | flops 128 | bytes 1024
  21.2 240.8 %conditional.4 = (bf16[640,512]{1,0:T(8,128)(2,1)S(1)}) conditional(s32[]{:T(128)} %clamp.3, (bf16[640,4096]{1,0:T(8,128)(2,1)}, bf16[4096,1024]{1,0:T(8,128)(2,1)}, s32[1,4]{1,0:T(1,128)}, bf16[4,4096,128]{2,1,0:T(8,128)(2,1)}, bf16[4,128,512]{2,1,0:T(8,128)(2,1)}, /*index=5*/s32[2,8,8]{2,1,0:T(8,128)S(1)}, ...), branch_computations={%region_20.42_spmd, %region_42.64_spmd, %region_64.86_spmd, %regio... | conditional | flops 103621156864 | bytes 599829760
  29.7 7.6 %copy.75 = bf16[4,4096,128]{2,0,1:T(4,128)(2,1)} copy(bf16[4,4096,128]{2,1,0:T(8,128)(2,1)} %get-tuple-element.388) | data formatting | bytes 8388608 | tf_op jit(solution)/shard_map
  37.3 7.2 %reshape.1625 = bf16[2,2048,512]{2,1,0:T(8,128)(2,1)} reshape(bf16[4096,4,128]{2,1,0:T(4,128)(2,1)} %bitcast.827) | data formatting | bytes 8388608 | tf_op jit(solution)/shard_map/cond/branch_2_fun/reshape | solution.py:147
  44.5 4.5 %constant_dynamic-update-slice_fusion.5 = bf16[2,2304,512]{2,1,0:T(8,128)(2,1)} fusion(bf16[2,2048,512]{2,1,0:T(8,128)(2,1)} %reshape.1625), kind=kLoop, calls=%fused_computation.670 | loop fusion | bytes 8388608
  50.4 3.3 %dynamic-slice_bitcast_fusion.2 = bf16[2304,512]{1,0:T(8,128)(2,1)} fusion(bf16[2,2304,512]{2,1,0:T(8,128)(2,1)} %constant_dynamic-update-slice_fusion.4, s32[]{:T(128)S(6)} %select_n.1142), kind=kLoop, calls=%fused_computation.563 | loop fusion | bytes 4718596 | tf_op jit(solution)/shard_map/cond/branch_2_fun/jit(dynamic_index_in_dim)/squeeze | solution.py:151
  55.6 2.8 %collective-permute-done.41 = bf16[2304,512]{1,0:T(8,128)(2,1)S(1)} collective-permute-done((bf16[2304,512]{1,0:T(8,128)(2,1)}, bf16[2304,512]{1,0:T(8,128)(2,1)S(1)}, u32[]{:S(2)}, u32[]{:S(2)}) %collective-permute-start.41) | collective-permute-done | bytes 2359328 | tf_op jit(solution)/shard_map/cond/branch_2_fun/ppermute | solution.py:152
  58.4 2.0 bitcast_select_fusion.7
  60.3 4.2 %convolution_convert_fusion.8 = bf16[2304,768]{1,0:T(8,128)(2,1)S(1)} fusion(s32[768]{0:T(1024)S(1)} %broadcast_add_fusion.25, bf16[2304,512]{1,0:T(8,128)(2,1)S(1)} %get-tuple-element.586, bf16[2304,512]{1,0:T(8,128)(2,1)S(1)} %get-tuple-element.585), kind=kOutput, calls=%fused_computation.516 | convolution fusion | flops 3635871744 | bytes 8260608 | tf_op jit(solution)/shard_map/cond/branch_2_fun/dot_general | solution.py:98
  64.6 2.8 %collective-permute-start.42 = (bf16[384,768]{1,0:T(8,128)(2,1)S(1)}, bf16[384,768]{1,0:T(8,128)(2,1)S(1)}, u32[]{:S(2)}, u32[]{:S(2)}) collective-permute-start(bf16[384,768]{1,0:T(8,128)(2,1)S(1)} %constant_dynamic-slice_fusion.29), channel_id=1, source_target_pairs={{0,4},{2,6},{4,8},{6,10},{8,12},{10,14},{1,5},{3,7},{5,9},{7,11},{... | collective-permute-start | bytes 1769480 | tf_op jit(solution)/shard_map/cond/branch_2_fun/ppermute | solution.py:221
  67.4 4.2 %convolution_convert_fusion.7 = bf16[2304,768]{1,0:T(8,128)(2,1)S(1)} fusion(s32[768]{0:T(1024)S(1)} %broadcast_add_fusion.23, bf16[2304,512]{1,0:T(8,128)(2,1)S(1)} %get-tuple-element.586, bf16[2304,512]{1,0:T(8,128)(2,1)S(1)} %get-tuple-element.585), kind=kOutput, calls=%fused_computation.515 | convolution fusion | flops 3635871744 | bytes 8260608 | tf_op jit(solution)/shard_map/cond/branch_2_fun/dot_general | solution.py:98
  71.6 1.3 collective-permute-start.50
  73.0 7.3 %collective-permute-done.42 = bf16[384,768]{1,0:T(8,128)(2,1)S(1)} collective-permute-done((bf16[384,768]{1,0:T(8,128)(2,1)S(1)}, bf16[384,768]{1,0:T(8,128)(2,1)S(1)}, u32[]{:S(2)}, u32[]{:S(2)}) %collective-permute-start.42) | collective-permute-done | bytes 589856 | tf_op jit(solution)/shard_map/cond/branch_2_fun/ppermute | solution.py:221
  81.0 4.4 %collective-permute-start.43 = (bf16[384,768]{1,0:T(8,128)(2,1)S(1)}, bf16[384,768]{1,0:T(8,128)(2,1)S(1)}, u32[]{:S(2)}, u32[]{:S(2)}) collective-permute-start(bf16[384,768]{1,0:T(8,128)(2,1)S(1)} %add_convert_fusion.41), channel_id=1, source_target_pairs={{0,4},{2,6},{4,8},{6,10},{8,12},{10,14},{1,5},{3,7},{5,9},{7,11},{... | collective-permute-start | bytes 1769480 | tf_op jit(solution)/shard_map/cond/branch_2_fun/ppermute | solution.py:221
  85.4 3.2 %collective-permute-done.50 = bf16[384,768]{1,0:T(8,128)(2,1)S(1)} collective-permute-done((bf16[384,768]{1,0:T(8,128)(2,1)S(1)}, bf16[384,768]{1,0:T(8,128)(2,1)S(1)}, u32[]{:S(2)}, u32[]{:S(2)}) %collective-permute-start.50) | collective-permute-done | bytes 589856 | tf_op jit(solution)/shard_map/cond/branch_2_fun/ppermute | solution.py:222
  89.4 1.3 collective-permute-start.51
  90.7 0.9 fusion.344
  92.4 5.0 %collective-permute-done.43 = bf16[384,768]{1,0:T(8,128)(2,1)S(1)} collective-permute-done((bf16[384,768]{1,0:T(8,128)(2,1)S(1)}, bf16[384,768]{1,0:T(8,128)(2,1)S(1)}, u32[]{:S(2)}, u32[]{:S(2)}) %collective-permute-start.43) | collective-permute-done | bytes 589856 | tf_op jit(solution)/shard_map/cond/branch_2_fun/ppermute | solution.py:221
  98.2 4.6 %collective-permute-start.44 = (bf16[384,768]{1,0:T(8,128)(2,1)S(1)}, bf16[384,768]{1,0:T(8,128)(2,1)S(1)}, u32[]{:S(2)}, u32[]{:S(2)}) collective-permute-start(bf16[384,768]{1,0:T(8,128)(2,1)S(1)} %add_convert_fusion.40), channel_id=1, source_target_pairs={{0,4},{2,6},{4,8},{6,10},{8,12},{10,14},{1,5},{3,7},{5,9},{7,11},{... | collective-permute-start | bytes 1769480 | tf_op jit(solution)/shard_map/cond/branch_2_fun/ppermute | solution.py:221
  102.8 2.7 %collective-permute-done.51 = bf16[384,768]{1,0:T(8,128)(2,1)S(1)} collective-permute-done((bf16[384,768]{1,0:T(8,128)(2,1)S(1)}, bf16[384,768]{1,0:T(8,128)(2,1)S(1)}, u32[]{:S(2)}, u32[]{:S(2)}) %collective-permute-start.51) | collective-permute-done | bytes 589856 | tf_op jit(solution)/shard_map/cond/branch_2_fun/ppermute | solution.py:222
  106.2 1.3 collective-permute-start.52
  107.5 0.9 fusion.346
  108.4 0.9 fusion.362
  109.3 4.4 %collective-permute-done.44 = bf16[384,768]{1,0:T(8,128)(2,1)S(1)} collective-permute-done((bf16[384,768]{1,0:T(8,128)(2,1)S(1)}, bf16[384,768]{1,0:T(8,128)(2,1)S(1)}, u32[]{:S(2)}, u32[]{:S(2)}) %collective-permute-start.44) | collective-permute-done | bytes 589856 | tf_op jit(solution)/shard_map/cond/branch_2_fun/ppermute | solution.py:221
  114.4 4.4 %collective-permute-start.45 = (bf16[384,768]{1,0:T(8,128)(2,1)S(1)}, bf16[384,768]{1,0:T(8,128)(2,1)S(1)}, u32[]{:S(2)}, u32[]{:S(2)}) collective-permute-start(bf16[384,768]{1,0:T(8,128)(2,1)S(1)} %add_convert_fusion.39), channel_id=1, source_target_pairs={{0,4},{2,6},{4,8},{6,10},{8,12},{10,14},{1,5},{3,7},{5,9},{7,11},{... | collective-permute-start | bytes 1769480 | tf_op jit(solution)/shard_map/cond/branch_2_fun/ppermute | solution.py:221
  118.8 2.6 collective-permute-done.52
  122.2 1.3 collective-permute-start.53
  124.3 0.9 fusion.364
  125.2 3.8 %collective-permute-done.45 = bf16[384,768]{1,0:T(8,128)(2,1)S(1)} collective-permute-done((bf16[384,768]{1,0:T(8,128)(2,1)S(1)}, bf16[384,768]{1,0:T(8,128)(2,1)S(1)}, u32[]{:S(2)}, u32[]{:S(2)}) %collective-permute-start.45) | collective-permute-done | bytes 589856 | tf_op jit(solution)/shard_map/cond/branch_2_fun/ppermute | solution.py:221
  129.7 4.4 %collective-permute-start.46 = (bf16[384,768]{1,0:T(8,128)(2,1)S(1)}, bf16[384,768]{1,0:T(8,128)(2,1)S(1)}, u32[]{:S(2)}, u32[]{:S(2)}) collective-permute-start(bf16[384,768]{1,0:T(8,128)(2,1)S(1)} %add_convert_fusion.38), channel_id=1, source_target_pairs={{0,4},{2,6},{4,8},{6,10},{8,12},{10,14},{1,5},{3,7},{5,9},{7,11},{... | collective-permute-start | bytes 1769480 | tf_op jit(solution)/shard_map/cond/branch_2_fun/ppermute | solution.py:221
  134.2 2.3 collective-permute-done.53
  137.2 1.3 collective-permute-start.54
  139.3 0.9 fusion.366
  140.2 3.2 %collective-permute-done.46 = bf16[384,768]{1,0:T(8,128)(2,1)S(1)} collective-permute-done((bf16[384,768]{1,0:T(8,128)(2,1)S(1)}, bf16[384,768]{1,0:T(8,128)(2,1)S(1)}, u32[]{:S(2)}, u32[]{:S(2)}) %collective-permute-start.46) | collective-permute-done | bytes 589856 | tf_op jit(solution)/shard_map/cond/branch_2_fun/ppermute | solution.py:221
  144.1 4.4 %collective-permute-start.47 = (bf16[384,768]{1,0:T(8,128)(2,1)S(1)}, bf16[384,768]{1,0:T(8,128)(2,1)S(1)}, u32[]{:S(2)}, u32[]{:S(2)}) collective-permute-start(bf16[384,768]{1,0:T(8,128)(2,1)S(1)} %add_convert_fusion.37), channel_id=1, source_target_pairs={{0,4},{2,6},{4,8},{6,10},{8,12},{10,14},{1,5},{3,7},{5,9},{7,11},{... | collective-permute-start | bytes 1769480 | tf_op jit(solution)/shard_map/cond/branch_2_fun/ppermute | solution.py:221
  148.6 1.9 collective-permute-done.54
  151.3 1.7 collective-permute-start.55
  153.0 0.9 fusion.352
  153.8 0.9 fusion.368
  154.7 2.2 collective-permute-done.47
  157.6 4.4 %collective-permute-start.48 = (bf16[384,768]{1,0:T(8,128)(2,1)S(1)}, bf16[384,768]{1,0:T(8,128)(2,1)S(1)}, u32[]{:S(2)}, u32[]{:S(2)}) collective-permute-start(bf16[384,768]{1,0:T(8,128)(2,1)S(1)} %add_convert_fusion.36), channel_id=1, source_target_pairs={{0,4},{2,6},{4,8},{6,10},{8,12},{10,14},{1,5},{3,7},{5,9},{7,11},{... | collective-permute-start | bytes 1769480 | tf_op jit(solution)/shard_map/cond/branch_2_fun/ppermute | solution.py:221
  162.1 1.8 collective-permute-done.55
  164.6 1.3 collective-permute-start.56
  167.6 2.6 collective-permute-done.48
  171.0 4.4 %collective-permute-start.49 = (bf16[384,768]{1,0:T(8,128)(2,1)S(1)}, bf16[384,768]{1,0:T(8,128)(2,1)S(1)}, u32[]{:S(2)}, u32[]{:S(2)}) collective-permute-start(bf16[384,768]{1,0:T(8,128)(2,1)S(1)} %add_convert_fusion.35), channel_id=1, source_target_pairs={{0,4},{2,6},{4,8},{6,10},{8,12},{10,14},{1,5},{3,7},{5,9},{7,11},{... | collective-permute-start | bytes 1769480 | tf_op jit(solution)/shard_map/cond/branch_2_fun/ppermute | solution.py:221
  175.4 1.9 collective-permute-done.56
  178.1 1.3 collective-permute-start.57
  179.4 0.9 fusion.356
  180.2 0.9 fusion.372
  181.1 1.7 collective-permute-done.49
  183.6 6.2 %collective-permute-done.57 = bf16[384,768]{1,0:T(8,128)(2,1)S(1)} collective-permute-done((bf16[384,768]{1,0:T(8,128)(2,1)S(1)}, bf16[384,768]{1,0:T(8,128)(2,1)S(1)}, u32[]{:S(2)}, u32[]{:S(2)}) %collective-permute-start.57) | collective-permute-done | bytes 589856 | tf_op jit(solution)/shard_map/cond/branch_2_fun/ppermute | solution.py:222
  190.7 6.3 %select_add_fusion.2 = bf16[2304,1024]{1,0:T(8,128)(2,1)S(1)} fusion(bf16[3072,1024]{1,0:T(8,128)(2,1)S(1)} %fusion.374, s32[]{:T(128)S(6)} %select_n.1193, bf16[3072,1024]{1,0:T(8,128)(2,1)S(1)} %fusion.358, s32[]{:T(128)S(6)} %select_n.1173, pred[]{:T(512)S(6)} %lt.1249, pred[]{:T(512)S(6)} %gt.99, s32[1024]{0:T(1024)S(1)} %pad_add_fusion.6, ...), kind=kOutput, calls=%fused_computation.518 | convolution fusion | flops 4863557632 | bytes 18878474 | tf_op jit(solution)/shard_map/cond/branch_2_fun/dot_general | solution.py:98
  197.1 2.1 copy-done.7
  199.6 9.5 %fusion.770 = f32[640,1024]{1,0:T(8,128)S(1)} fusion(bf16[640,4096]{1,0:T(8,128)(2,1)} %get-tuple-element.195, bf16[4096,1024]{1,0:T(8,128)(2,1)} %get-tuple-element.200), kind=kOutput, calls=%fused_computation.1375 | convolution fusion | flops 5368709120 | bytes 16252928 | tf_op jit(solution)/shard_map/cond/branch_2_fun/dot_general | solution.py:225
  209.1 1.5 copy-done.19
  210.6 1.2 constant_dynamic-slice_fusion.32
  211.8 1.4 collective-permute-start.40
  213.6 2.8 %broadcast_select_fusion.5 = (bf16[2304,512]{1,0:T(8,128)(2,1)S(1)}, bf16[2304,512]{1,0:T(8,128)(2,1)S(1)}) fusion(bf16[2304,512]{1,0:T(8,128)(2,1)} %collective-permute-done.58, pred[]{:T(512)S(6)} %eq.446, bf16[2304,1024]{1,0:T(8,128)(2,1)} %copy-done.7), kind=kLoop, calls=%fused_computation.565 | loop fusion | flops 2359296 | bytes 9437185 | tf_op jit(solution)/shard_map/cond/branch_2_fun/jit(_where)/select_n | solution.py:244
  217.5 1.8 fusion.304
  219.3 1.9 fusion.375
  222.1 1.1 slice.181
  223.3 26.9 %collective-permute-done.59 = f32[640,128]{0,1:T(8,128)S(1)} collective-permute-done((f32[640,128]{0,1:T(8,128)S(1)}, f32[640,128]{0,1:T(8,128)S(1)}, u32[]{:S(2)}, u32[]{:S(2)}) %collective-permute-start.59) | collective-permute-done | bytes 327712 | tf_op jit(solution)/shard_map/cond/branch_2_fun/ppermute | solution.py:104
  250.5 1.9 add_add_fusion.2
  (125 shorter events, 27.2 us)
Async XLA Ops:
  44.5 4.5 %copy-start.2 = (bf16[4,128,512]{2,1,0:T(8,128)(2,1)S(1)}, bf16[4,128,512]{2,1,0:T(8,128)(2,1)}, u32[]{:S(2)}) copy-start(bf16[4,128,512]{2,1,0:T(8,128)(2,1)} %get-tuple-element.389) | copy-start | bytes 1572868
  49.5 4.8 %copy-start.49 = (s32[32]{0:T(128)S(1)}, s32[32]{0:T(128)}, u32[]{:S(2)}) copy-start(s32[32]{0:T(128)} %get-tuple-element.131) | copy-start | bytes 388
  53.6 4.7 %collective-permute-start.41 = (bf16[2304,512]{1,0:T(8,128)(2,1)}, bf16[2304,512]{1,0:T(8,128)(2,1)S(1)}, u32[]{:S(2)}, u32[]{:S(2)}) collective-permute-start(bf16[2304,512]{1,0:T(8,128)(2,1)} %dynamic-slice_bitcast_fusion.2), channel_id=1, source_target_pairs={{0,2},{2,0},{4,6},{6,4},{8,10},{10,8},{12,14},{14,12},{1,3},{3,1},... | collective-permute-start | bytes 7077896 | tf_op jit(solution)/shard_map/cond/branch_2_fun/ppermute | solution.py:152
  64.6 15.7 %collective-permute-start.42 = (bf16[384,768]{1,0:T(8,128)(2,1)S(1)}, bf16[384,768]{1,0:T(8,128)(2,1)S(1)}, u32[]{:S(2)}, u32[]{:S(2)}) collective-permute-start(bf16[384,768]{1,0:T(8,128)(2,1)S(1)} %constant_dynamic-slice_fusion.29), channel_id=1, source_target_pairs={{0,4},{2,6},{4,8},{6,10},{8,12},{10,14},{1,5},{3,7},{5,9},{7,11},{... | collective-permute-start | bytes 1769480 | tf_op jit(solution)/shard_map/cond/branch_2_fun/ppermute | solution.py:221
  71.6 17.0 %collective-permute-start.50 = (bf16[384,768]{1,0:T(8,128)(2,1)S(1)}, bf16[384,768]{1,0:T(8,128)(2,1)S(1)}, u32[]{:S(2)}, u32[]{:S(2)}) collective-permute-start(bf16[384,768]{1,0:T(8,128)(2,1)S(1)} %constant_dynamic-slice_fusion.25), channel_id=1, source_target_pairs={{4,0},{6,2},{8,4},{10,6},{12,8},{14,10},{5,1},{7,3},{9,5},{11,7},{... | collective-permute-start | bytes 1769480 | tf_op jit(solution)/shard_map/cond/branch_2_fun/ppermute | solution.py:222
  81.0 16.4 %collective-permute-start.43 = (bf16[384,768]{1,0:T(8,128)(2,1)S(1)}, bf16[384,768]{1,0:T(8,128)(2,1)S(1)}, u32[]{:S(2)}, u32[]{:S(2)}) collective-permute-start(bf16[384,768]{1,0:T(8,128)(2,1)S(1)} %add_convert_fusion.41), channel_id=1, source_target_pairs={{0,4},{2,6},{4,8},{6,10},{8,12},{10,14},{1,5},{3,7},{5,9},{7,11},{... | collective-permute-start | bytes 1769480 | tf_op jit(solution)/shard_map/cond/branch_2_fun/ppermute | solution.py:221
  89.4 16.1 %collective-permute-start.51 = (bf16[384,768]{1,0:T(8,128)(2,1)S(1)}, bf16[384,768]{1,0:T(8,128)(2,1)S(1)}, u32[]{:S(2)}, u32[]{:S(2)}) collective-permute-start(bf16[384,768]{1,0:T(8,128)(2,1)S(1)} %add_convert_fusion.34), channel_id=1, source_target_pairs={{4,0},{6,2},{8,4},{10,6},{12,8},{14,10},{5,1},{7,3},{9,5},{11,7},{... | collective-permute-start | bytes 1769480 | tf_op jit(solution)/shard_map/cond/branch_2_fun/ppermute | solution.py:222
  98.2 15.5 %collective-permute-start.44 = (bf16[384,768]{1,0:T(8,128)(2,1)S(1)}, bf16[384,768]{1,0:T(8,128)(2,1)S(1)}, u32[]{:S(2)}, u32[]{:S(2)}) collective-permute-start(bf16[384,768]{1,0:T(8,128)(2,1)S(1)} %add_convert_fusion.40), channel_id=1, source_target_pairs={{0,4},{2,6},{4,8},{6,10},{8,12},{10,14},{1,5},{3,7},{5,9},{7,11},{... | collective-permute-start | bytes 1769480 | tf_op jit(solution)/shard_map/cond/branch_2_fun/ppermute | solution.py:221
  106.2 15.2 %collective-permute-start.52 = (bf16[384,768]{1,0:T(8,128)(2,1)S(1)}, bf16[384,768]{1,0:T(8,128)(2,1)S(1)}, u32[]{:S(2)}, u32[]{:S(2)}) collective-permute-start(bf16[384,768]{1,0:T(8,128)(2,1)S(1)} %add_convert_fusion.33), channel_id=1, source_target_pairs={{4,0},{6,2},{8,4},{10,6},{12,8},{14,10},{5,1},{7,3},{9,5},{11,7},{... | collective-permute-start | bytes 1769480 | tf_op jit(solution)/shard_map/cond/branch_2_fun/ppermute | solution.py:222
  114.4 14.6 %collective-permute-start.45 = (bf16[384,768]{1,0:T(8,128)(2,1)S(1)}, bf16[384,768]{1,0:T(8,128)(2,1)S(1)}, u32[]{:S(2)}, u32[]{:S(2)}) collective-permute-start(bf16[384,768]{1,0:T(8,128)(2,1)S(1)} %add_convert_fusion.39), channel_id=1, source_target_pairs={{0,4},{2,6},{4,8},{6,10},{8,12},{10,14},{1,5},{3,7},{5,9},{7,11},{... | collective-permute-start | bytes 1769480 | tf_op jit(solution)/shard_map/cond/branch_2_fun/ppermute | solution.py:221
  122.2 14.3 %collective-permute-start.53 = (bf16[384,768]{1,0:T(8,128)(2,1)S(1)}, bf16[384,768]{1,0:T(8,128)(2,1)S(1)}, u32[]{:S(2)}, u32[]{:S(2)}) collective-permute-start(bf16[384,768]{1,0:T(8,128)(2,1)S(1)} %add_convert_fusion.32), channel_id=1, source_target_pairs={{4,0},{6,2},{8,4},{10,6},{12,8},{14,10},{5,1},{7,3},{9,5},{11,7},{... | collective-permute-start | bytes 1769480 | tf_op jit(solution)/shard_map/cond/branch_2_fun/ppermute | solution.py:222
  129.7 13.7 %collective-permute-start.46 = (bf16[384,768]{1,0:T(8,128)(2,1)S(1)}, bf16[384,768]{1,0:T(8,128)(2,1)S(1)}, u32[]{:S(2)}, u32[]{:S(2)}) collective-permute-start(bf16[384,768]{1,0:T(8,128)(2,1)S(1)} %add_convert_fusion.38), channel_id=1, source_target_pairs={{0,4},{2,6},{4,8},{6,10},{8,12},{10,14},{1,5},{3,7},{5,9},{7,11},{... | collective-permute-start | bytes 1769480 | tf_op jit(solution)/shard_map/cond/branch_2_fun/ppermute | solution.py:221
  137.2 13.3 %collective-permute-start.54 = (bf16[384,768]{1,0:T(8,128)(2,1)S(1)}, bf16[384,768]{1,0:T(8,128)(2,1)S(1)}, u32[]{:S(2)}, u32[]{:S(2)}) collective-permute-start(bf16[384,768]{1,0:T(8,128)(2,1)S(1)} %add_convert_fusion.31), channel_id=1, source_target_pairs={{4,0},{6,2},{8,4},{10,6},{12,8},{14,10},{5,1},{7,3},{9,5},{11,7},{... | collective-permute-start | bytes 1769480 | tf_op jit(solution)/shard_map/cond/branch_2_fun/ppermute | solution.py:222
  144.1 12.7 %collective-permute-start.47 = (bf16[384,768]{1,0:T(8,128)(2,1)S(1)}, bf16[384,768]{1,0:T(8,128)(2,1)S(1)}, u32[]{:S(2)}, u32[]{:S(2)}) collective-permute-start(bf16[384,768]{1,0:T(8,128)(2,1)S(1)} %add_convert_fusion.37), channel_id=1, source_target_pairs={{0,4},{2,6},{4,8},{6,10},{8,12},{10,14},{1,5},{3,7},{5,9},{7,11},{... | collective-permute-start | bytes 1769480 | tf_op jit(solution)/shard_map/cond/branch_2_fun/ppermute | solution.py:221
  151.3 12.6 %collective-permute-start.55 = (bf16[384,768]{1,0:T(8,128)(2,1)S(1)}, bf16[384,768]{1,0:T(8,128)(2,1)S(1)}, u32[]{:S(2)}, u32[]{:S(2)}) collective-permute-start(bf16[384,768]{1,0:T(8,128)(2,1)S(1)} %add_convert_fusion.30), channel_id=1, source_target_pairs={{4,0},{6,2},{8,4},{10,6},{12,8},{14,10},{5,1},{7,3},{9,5},{11,7},{... | collective-permute-start | bytes 1769480 | tf_op jit(solution)/shard_map/cond/branch_2_fun/ppermute | solution.py:222
  157.6 12.6 %collective-permute-start.48 = (bf16[384,768]{1,0:T(8,128)(2,1)S(1)}, bf16[384,768]{1,0:T(8,128)(2,1)S(1)}, u32[]{:S(2)}, u32[]{:S(2)}) collective-permute-start(bf16[384,768]{1,0:T(8,128)(2,1)S(1)} %add_convert_fusion.36), channel_id=1, source_target_pairs={{0,4},{2,6},{4,8},{6,10},{8,12},{10,14},{1,5},{3,7},{5,9},{7,11},{... | collective-permute-start | bytes 1769480 | tf_op jit(solution)/shard_map/cond/branch_2_fun/ppermute | solution.py:221
  164.6 12.7 %collective-permute-start.56 = (bf16[384,768]{1,0:T(8,128)(2,1)S(1)}, bf16[384,768]{1,0:T(8,128)(2,1)S(1)}, u32[]{:S(2)}, u32[]{:S(2)}) collective-permute-start(bf16[384,768]{1,0:T(8,128)(2,1)S(1)} %add_convert_fusion.29), channel_id=1, source_target_pairs={{4,0},{6,2},{8,4},{10,6},{12,8},{14,10},{5,1},{7,3},{9,5},{11,7},{... | collective-permute-start | bytes 1769480 | tf_op jit(solution)/shard_map/cond/branch_2_fun/ppermute | solution.py:222
  171.0 11.8 %collective-permute-start.49 = (bf16[384,768]{1,0:T(8,128)(2,1)S(1)}, bf16[384,768]{1,0:T(8,128)(2,1)S(1)}, u32[]{:S(2)}, u32[]{:S(2)}) collective-permute-start(bf16[384,768]{1,0:T(8,128)(2,1)S(1)} %add_convert_fusion.35), channel_id=1, source_target_pairs={{0,4},{2,6},{4,8},{6,10},{8,12},{10,14},{1,5},{3,7},{5,9},{7,11},{... | collective-permute-start | bytes 1769480 | tf_op jit(solution)/shard_map/cond/branch_2_fun/ppermute | solution.py:221
  178.1 11.8 %collective-permute-start.57 = (bf16[384,768]{1,0:T(8,128)(2,1)S(1)}, bf16[384,768]{1,0:T(8,128)(2,1)S(1)}, u32[]{:S(2)}, u32[]{:S(2)}) collective-permute-start(bf16[384,768]{1,0:T(8,128)(2,1)S(1)} %add_convert_fusion.28), channel_id=1, source_target_pairs={{4,0},{6,2},{8,4},{10,6},{12,8},{14,10},{5,1},{7,3},{9,5},{11,7},{... | collective-permute-start | bytes 1769480 | tf_op jit(solution)/shard_map/cond/branch_2_fun/ppermute | solution.py:222
  197.1 2.1 copy-start.7
  199.5 14.1 %collective-permute-start.58 = (bf16[2304,512]{1,0:T(8,128)(2,1)S(1)}, bf16[2304,512]{1,0:T(8,128)(2,1)}, u32[]{:S(2)}, u32[]{:S(2)}) collective-permute-start(bf16[2304,512]{1,0:T(8,128)(2,1)S(1)} %slice.178), channel_id=1, source_target_pairs={{0,2},{2,0},{4,6},{6,4},{8,10},{10,8},{12,14},{14,12},{1,3},{3,1},... | collective-permute-start | bytes 7077896 | tf_op jit(solution)/shard_map/cond/branch_2_fun/ppermute | solution.py:243
  199.6 13.7 %copy-start.55 = (s32[1,4]{1,0:T(1,128)S(1)}, s32[1,4]{1,0:T(1,128)}, u32[]{:S(2)}) copy-start(s32[1,4]{1,0:T(1,128)} %get-tuple-element.245) | copy-start | bytes 52
  209.1 1.5 copy-start.19
  211.8 38.6 %collective-permute-start.40 = (f32[640,512]{1,0:T(8,128)}, f32[640,512]{1,0:T(8,128)}, u32[]{:S(2)}, u32[]{:S(2)}) collective-permute-start(f32[640,512]{1,0:T(8,128)} %constant_dynamic-slice_fusion.32), channel_id=1, source_target_pairs={{0,1},{1,0},{2,3},{3,2},{4,5},{5,4},{6,7},{7,6},{8,9},{9,8},{10,11... | collective-permute-start | bytes 3932168 | tf_op jit(solution)/shard_map/cond/branch_2_fun/ppermute | solution.py:230
  213.5 3.6 %slice-start.12 = ((s8[5242880]{0:T(1024)(128)(4,1)}), s8[4194304]{0:T(1024)(128)(4,1)S(1)}, s32[]{:S(2)}) async-start(s8[5242880]{0:T(1024)(128)(4,1)} %bitcast.871), calls=%async_computation.12 | async-start | bytes 8388608
  213.5 3.9 %slice-start.13 = ((s8[5242880]{0:T(1024)(128)(4,1)}), s8[1048576]{0:T(1024)(128)(4,1)S(1)}, s32[]{:S(2)}) async-start(s8[5242880]{0:T(1024)(128)(4,1)} %bitcast.871), calls=%async_computation.13 | async-start | bytes 2097152
  216.4 2.9 %copy-start.12 = (bf16[2304,512]{1,0:T(8,128)(2,1)}, bf16[2304,512]{1,0:T(8,128)(2,1)S(1)}, u32[]{:S(2)}) copy-start(bf16[2304,512]{1,0:T(8,128)(2,1)S(1)} %get-tuple-element.583) | copy-start | bytes 7077892
  221.3 28.9 %collective-permute-start.59 = (f32[640,128]{0,1:T(8,128)S(1)}, f32[640,128]{0,1:T(8,128)S(1)}, u32[]{:S(2)}, u32[]{:S(2)}) collective-permute-start(f32[640,128]{0,1:T(8,128)S(1)} %select_reduce_fusion.36), channel_id=1, source_target_pairs={{0,1},{1,0},{2,3},{3,2},{4,5},{5,4},{6,7},{7,6},{8,9},{9,8},{10,11... | collective-permute-start | bytes 983048 | tf_op jit(solution)/shard_map/cond/branch_2_fun/ppermute | solution.py:104
  222.0 28.5 %copy-start.20 = (f32[640,1024]{1,0:T(8,128)S(1)}, f32[640,1024]{1,0:T(8,128)}, u32[]{:S(2)}) copy-start(f32[640,1024]{1,0:T(8,128)} %copy-done.19) | copy-start | bytes 7864324
  261.9 0.8 copy-start.33
